TPU v7x, 32 devices: a whole 2x2x4 slice. The times are simulated.
32 devices in a mesh: groups: 2 (over y), tm: 4 (over z), cols: 4 (over x, core).
Axes of the slice: x: 2, y: 2, z: 4, core: 2. Of those that a mesh axis runs over, the one named last changes fastest.
Arguments:
- latent: bfloat16 [8, 48, 128, 256], P(('groups', 'tm'), None, 'cols'), parts along dimension 0, may hold values from -6 to 6
- spatial_one: bfloat16 [3, 3, 256, 256], replicated, may hold values from -0.125 to 0.125
- bias_one: float32 [256], replicated, may hold values from -3 to 3
- spatial_two: bfloat16 [3, 3, 256, 256], replicated, may hold values from -0.125 to 0.125
- bias_two: float32 [256], replicated, may hold values from -3 to 3
- temporal_one: bfloat16 [3, 256, 256], replicated, may hold values from -0.75 to 0.75
- tbias_one: float32 [256], replicated, may hold values from -3 to 3
- temporal_two: bfloat16 [3, 256, 256], replicated, may hold values from -0.75 to 0.75
- tbias_two: float32 [256], replicated, may hold values from -3 to 3
Outputs:
- act_one: bfloat16 [8, 48, 128, 256], P(('groups', 'tm'), None, 'cols'), parts along dimension 0
- act_two: bfloat16 [8, 48, 128, 256], P(('groups', 'tm'), None, 'cols'), parts along dimension 0
- act_three: bfloat16 [8, 48, 128, 256], P(('groups', 'tm'), None, 'cols'), parts along dimension 0
- act_four: bfloat16 [8, 48, 128, 256], P(('groups', 'tm'), None, 'cols'), parts along dimension 0
There are 2 independent parts, one for each index of `groups`. A program takes and returns all parts, laid end to end along the dimension named above; an argument that names none is the same for every part. Nothing has to cross between parts.
All inputs are finite; a program needn't handle non-finite values.
Results may differ from a plain program's by a relative error of at most 0.012.
Values may be sent and summed in bfloat16 or wider, within the bound.
A program may use at most 64 MiB of HBM per device.

v0:
```python
import functools

import jax
import jax.numpy as jnp
from jax import lax
from jax.experimental import pallas as pl
from jax.experimental.pallas import tpu as pltpu
from jax.sharding import PartitionSpec as P

MESH = pl.DeviceIdType.MESH
TILE = 16
LAG = 3
EARLY = 0
HALO_LAG = 2
ROWS = 4
PIECES = 2
VMEM_BYTES = 58 * 1024 * 1024


def silu(values):
    half = 0.5 * values.astype(jnp.float32)
    return half + half * jnp.tanh(half)


def mm(a, b):
    return jnp.dot(a, b, preferred_element_type=jnp.float32)


def kernel(
    n, n_cols, R, hops,
    *refs,
):
    given, outs, held = refs[:9], refs[9:13], refs[13:22]
    hal1, hal2, s1, s2, x2in, qs, ps, qr, pr, a1, a2, a3, a4 = refs[22:35]
    h_send, h_recv, z_send, z_recv, q_send, q_recv, i_sem, o_sem = refs[35:]
    x_held, k1, b1, k2, b2, u, tb1, v, tb2 = held

    k = lax.axis_index("tm")
    c = lax.axis_index("cols")
    rows, W, C = a1.shape
    loads = [pltpu.make_async_copy(given[i], held[i], i_sem.at[i]) for i in range(9)]
    for load_in in loads:
        load_in.start()
    chunks = rows // R
    M = R * W
    last = n - 1
    x = x_held.at[0]
    x_hbm = given[0].at[0]

    def cut(j):
        return pl.ds(j * R, R)

    partners = [(c > 0, {"cols": c - 1}), (c < n_cols - 1, {"cols": c + 1})]
    for h in range(1, hops + 1):
        partners.append((k + h < last, {"tm": k + h}))
        partners.append(((k - h >= 0) & (k < last), {"tm": k - h}))
    if n > 1:
        partners.append((k == last - 1, {"tm": k + 1}))
        partners.append((k == last, {"tm": k - 1}))
    barrier = pltpu.get_barrier_semaphore()
    count = jnp.int32(0)
    for there, device in partners:
        count = count + there.astype(jnp.int32)

        @pl.when(there)
        def _():
            pl.semaphore_signal(barrier, inc=1, device_id=device, device_id_type=MESH)

    edge = jnp.zeros((rows, TILE, C), jnp.bfloat16)

    @pl.when(c == 0)
    def _():
        hal1[0] = edge
        hal2[0] = edge

    @pl.when(c == n_cols - 1)
    def _():
        hal1[1] = edge
        hal2[1] = edge

    for s in (s1, s2):
        s[0] = jnp.zeros(s.shape[1:], s.dtype)
        s[rows + 1] = jnp.zeros(s.shape[1:], s.dtype)
    for h in range(1, hops + 1):

        @pl.when((k < h) & (k < last))
        def _():
            x2in[h - 1] = jnp.zeros(x2in.shape[1:], x2in.dtype)

    pl.semaphore_wait(barrier, count)

    def halo(layer, side, j):
        src = a1 if layer else x_hbm
        dst = hal2 if layer else hal1
        tile = pl.ds(W - TILE, TILE) if side == 0 else pl.ds(0, TILE)
        return pltpu.make_async_remote_copy(
            src_ref=src.at[cut(j), tile, :],
            dst_ref=dst.at[side, cut(j)],
            send_sem=h_send.at[layer, side, j],
            recv_sem=h_recv.at[layer, side, j],
            device_id={"cols": c + 1 if side == 0 else c - 1},
            device_id_type=MESH,
        )

    def halo_sends(layer, j, act):
        @pl.when(c < n_cols - 1)
        def _():
            act(halo(layer, 0, j))

        @pl.when(c > 0)
        def _():
            act(halo(layer, 1, j))

    def halo_waits(layer, j):
        @pl.when(c > 0)
        def _():
            halo(layer, 0, j).wait_recv()

        @pl.when(c < n_cols - 1)
        def _():
            halo(layer, 1, j).wait_recv()

    def frame_copy(h, j):
        return pltpu.make_async_remote_copy(
            src_ref=a2.at[cut(j)],
            dst_ref=x2in.at[h - 1, cut(j)],
            send_sem=z_send.at[h - 1, j],
            recv_sem=z_recv.at[h - 1, j],
            device_id={"tm": k + h},
            device_id_type=MESH,
        )

    def frame_sends(j, act):
        for h in range(1, hops + 1):

            @pl.when(k + h < last)
            def _():
                act(frame_copy(h, j))

    def part_copy(which, j):
        return pltpu.make_async_remote_copy(
            src_ref=(ps if which else qs).at[cut(j)],
            dst_ref=(pr if which else qr).at[cut(j)],
            send_sem=q_send.at[which, j],
            recv_sem=q_recv.at[which, j],
            device_id={"tm": k + 1},
            device_id_type=MESH,
        )

    def out_copy(which, j):
        src = (a1, a2, a3, a4)[which]
        return pltpu.make_async_copy(src.at[cut(j)], outs[which].at[0, cut(j)], o_sem.at[which, j])

    def build(layer, j):
        src, hal, dst = (a1, hal2, s2) if layer else (x, hal1, s1)
        mid = silu(src[cut(j)])
        left = silu(hal[0, cut(j)][:, TILE - 1 :, :])
        right = silu(hal[1, cut(j)][:, :1, :])
        here = pl.ds(j * R + 1, R)
        dst[here, :, 0:C] = jnp.concatenate([left, mid[:, : W - 1]], axis=1).astype(jnp.bfloat16)
        dst[here, :, C : 2 * C] = mid.astype(jnp.bfloat16)
        dst[here, :, 2 * C : 3 * C] = jnp.concatenate([mid[:, 1:], right], axis=1).astype(jnp.bfloat16)

    def conv(layer, j):
        src, s, kern, bias, dst = (a1, s2, k2, b2, a2) if layer else (x, s1, k1, b1, a1)
        acc = src[cut(j)].reshape(M, C).astype(jnp.float32) + bias[...][None, :]
        for dr in range(3):
            acc = acc + mm(s[pl.ds(j * R + dr, R)].reshape(M, 3 * C), kern[dr])
        dst[cut(j)] = acc.astype(jnp.bfloat16).reshape(R, W, C)

    def load(ref):
        return ref.reshape(M, C)

    def act(values):
        return silu(values).astype(jnp.bfloat16)

    def temporal_own(j):
        def arrive(h):
            @pl.when(k >= h)
            def _():
                frame_copy(h, j).wait_recv()

        x2 = [load(a2[cut(j)])]
        if hops > 0:
            arrive(1)
            x2.append(load(x2in[0, cut(j)]))
        t2 = [act(values) for values in x2]

        @pl.when(k == last - 1)
        def _():
            part = mm(t2[0], u[1])
            if hops > 0:
                part = part + mm(t2[1], u[0])
            qs[cut(j)] = part.astype(jnp.bfloat16).reshape(R, W, C)
            part_copy(0, j).start()

        for h in range(2, hops + 1):
            arrive(h)
            x2.append(load(x2in[h - 1, cut(j)]))
            t2.append(act(x2[h]))
        x3 = []
        for i in range(min(3, hops + 1)):
            total = x2[i].astype(jnp.float32) + tb1[...][None, :]
            for tap in range(3):
                if i + tap <= hops:
                    total = total + mm(t2[i + tap], u[2 - tap])
            if i > 0:
                total = jnp.where(k >= i, total, 0.0)
            x3.append(total.astype(jnp.bfloat16))
        t3 = [act(values) for values in x3]

        @pl.when(k == last - 1)
        def _():
            part = mm(t3[0], v[1])
            if len(t3) > 1:
                part = part + mm(t3[1], v[0])
            ps[cut(j)] = part.astype(jnp.bfloat16).reshape(R, W, C)
            part_copy(1, j).start()

        a3[cut(j)] = x3[0].reshape(R, W, C)
        out_copy(2, j).start()
        total = x3[0].astype(jnp.float32) + tb2[...][None, :]
        for tap in range(len(t3)):
            total = total + mm(t3[tap], v[2 - tap])
        a4[cut(j)] = total.astype(jnp.bfloat16).reshape(R, W, C)
        out_copy(3, j).start()

    def temporal_last(j):
        x2 = load(a2[cut(j)])
        total = x2.astype(jnp.float32) + mm(act(x2), u[2]) + tb1[...][None, :]
        if n > 1:
            part_copy(0, j).wait_recv()
            total = total + load(qr[cut(j)]).astype(jnp.float32)
        x3 = total.astype(jnp.bfloat16)
        a3[cut(j)] = x3.reshape(R, W, C)
        out_copy(2, j).start()
        total = x3.astype(jnp.float32) + mm(act(x3), v[2]) + tb2[...][None, :]
        if n > 1:
            part_copy(1, j).wait_recv()
            total = total + load(pr[cut(j)]).astype(jnp.float32)
        a4[cut(j)] = total.astype(jnp.bfloat16).reshape(R, W, C)
        out_copy(3, j).start()

    def start(copy):
        copy.start()

    @pl.loop(0, chunks)
    def _(j):
        halo_sends(0, j, start)

    def during(j, body):
        @pl.when((j >= 0) & (j < chunks))
        def _():
            body(j)

    def step_build1(j):
        halo_waits(0, j)
        build(0, j)

    def step_conv1(j):
        conv(0, j)
        halo_sends(1, j, start)
        out_copy(0, j).start()

    def step_build2(j):
        halo_waits(1, j)
        build(1, j)

    def step_conv2(j):
        conv(1, j)
        frame_sends(j, start)
        out_copy(1, j).start()

    def step_temporal(j):
        @pl.when(k < last)
        def _():
            temporal_own(j)

        @pl.when(k == last)
        def _():
            temporal_last(j)

    for load_in in loads:
        load_in.wait()
    lag = jnp.where(k == last - 1, EARLY, LAG)

    @pl.loop(0, chunks + 2 + HALO_LAG + LAG)
    def _(t):
        during(t, step_build1)
        during(t - 1, step_conv1)
        during(t - 1 - HALO_LAG, step_build2)
        during(t - 2 - HALO_LAG, step_conv2)
        during(t - 2 - HALO_LAG - lag, step_temporal)

    @pl.loop(0, chunks)
    def _(j):
        for layer in range(2):
            halo_sends(layer, j, lambda copy: copy.wait_send())
        frame_sends(j, lambda copy: copy.wait_send())
        for which in range(4):
            out_copy(which, j).wait()
        if n > 1:

            @pl.when(k == last - 1)
            def _():
                part_copy(0, j).wait_send()
                part_copy(1, j).wait_send()


def rows_per_chunk(rows):
    return max(r for r in range(1, ROWS + 1) if rows % r == 0)


def on_device(n, n_cols, latent, spatial_one, bias_one, spatial_two, bias_two, temporal_one, tbias_one, temporal_two, tbias_two):
    _, rows, W, C = latent.shape
    R = rows_per_chunk(rows)
    chunks = rows // R
    hops = max(0, min(4, n - 2))
    slots = max(1, hops)
    bf = jnp.bfloat16
    block = pltpu.VMEM((rows, W, C), bf)
    dma = pltpu.SemaphoreType.DMA
    anywhere = pl.BlockSpec(memory_space=pl.ANY)
    out = jax.ShapeDtypeStruct(latent.shape, bf)
    args = (
        latent,
        spatial_one.reshape(3, 3 * C, C), bias_one,
        spatial_two.reshape(3, 3 * C, C), bias_two,
        temporal_one, tbias_one, temporal_two, tbias_two,
    )
    results = pl.pallas_call(
        functools.partial(kernel, n, n_cols, R, hops),
        out_shape=(out,) * 4,
        in_specs=[anywhere] * 9,
        out_specs=(anywhere,) * 4,
        scratch_shapes=[
            *(pltpu.VMEM(arg.shape, arg.dtype) for arg in args),
            pltpu.VMEM((2, rows, TILE, C), bf),
            pltpu.VMEM((2, rows, TILE, C), bf),
            pltpu.VMEM((rows + 2, W, 3 * C), bf),
            pltpu.VMEM((rows + 2, W, 3 * C), bf),
            pltpu.VMEM((slots, rows, W, C), bf),
            block, block, block, block,
            block, block, block, block,
            dma((2, 2, chunks)), dma((2, 2, chunks)),
            dma((slots, chunks)), dma((slots, chunks)),
            dma((2, chunks)), dma((2, chunks)),
            dma((9,)), dma((4, chunks)),
        ],
        compiler_params=pltpu.CompilerParams(
            collective_id=0, has_side_effects=True, vmem_limit_bytes=VMEM_BYTES
        ),
    )(*args)
    return pl.pallas_call(
        write_out,
        out_shape=(out,) * 4,
        in_specs=[anywhere] * 4,
        out_specs=(anywhere,) * 4,
        scratch_shapes=[
            *(pltpu.VMEM(latent.shape, bf) for _ in range(4)),
            dma((4, PIECES)), dma((4, PIECES)),
        ],
        compiler_params=pltpu.CompilerParams(vmem_limit_bytes=VMEM_BYTES),
    )(*results)


def write_out(*refs):
    given, outs, held, i_sem, o_sem = refs[:4], refs[4:8], refs[8:12], refs[12], refs[13]
    rows = given[0].shape[1]
    ins, back = [], []
    for p in range(PIECES):
        part = pl.ds(rows * p // PIECES, rows * (p + 1) // PIECES - rows * p // PIECES)
        for i in range(4):
            ins.append(pltpu.make_async_copy(given[i].at[:, part], held[i].at[:, part], i_sem.at[i, p]))
            back.append(pltpu.make_async_copy(held[i].at[:, part], outs[i].at[:, part], o_sem.at[i, p]))
    for copy in ins:
        copy.start()
    for copy, after in zip(ins, back):
        copy.wait()
        after.start()
    for copy in back:
        copy.wait()


def solution(mesh):
    spec = P(("groups", "tm"), None, "cols", None)
    return jax.shard_map(
        functools.partial(on_device, mesh.shape["tm"], mesh.shape["cols"]),
        mesh=mesh,
        in_specs=(spec, P(), P(), P(), P(), P(), P(), P(), P()),
        out_specs=(spec,) * 4,
        check_vma=False,
    )
```

profile of v0, /device:TPU:25, one launch (start us, length us, event | category | flops | bytes accessed | tf_op | source)
XLA Modules:
  0.0 53.8 jit_solution(14706883527272210245)
XLA Ops:
  0.6 50.4 %shard_map.120 = (bf16[1,48,32,256]{3,2,1,0:T(8,128)(2,1)}, bf16[1,48,32,256]{3,2,1,0:T(8,128)(2,1)}, bf16[1,48,32,256]{3,2,1,0:T(8,128)(2,1)}, bf16[1,48,32,256]{3,2,1,0:T(8,128)(2,1)}) custom-call(bf16[1,48,32,256]{3,2,1,0:T(8,128)(2,1)} %refs_0_.1, bf16[3,768,256]{2,1,0:T(8,128)(2,1)} %bitcast.2, f32[256]{0:T(256)} %refs_2_.1, ...), custom_call_target="tpu_custom_call" | custom-call | tf_op jit(solution)/shard_map/pallas_call | solution.py:331
  51.0 2.8 %shard_map.121 = (bf16[1,48,32,256]{3,2,1,0:T(8,128)(2,1)}, bf16[1,48,32,256]{3,2,1,0:T(8,128)(2,1)}, bf16[1,48,32,256]{3,2,1,0:T(8,128)(2,1)}, bf16[1,48,32,256]{3,2,1,0:T(8,128)(2,1)}) custom-call(bf16[1,48,32,256]{3,2,1,0:T(8,128)(2,1)} %get-tuple-element.8.refs_0_, bf16[1,48,32,256]{3,2,1,0:T(8,128)(2,1)} %get-tuple-element.9.refs_1_, ...), custom_call_target="tpu_custom_call" | custom-call | tf_op jit(solution)/shard_map/pallas_call | solution.py:354
where the time goes:
time: 54 us; the launch traced here: 53.8 us
  Pallas kernels  53.2 us (99%)
  between operations  0.64 us (1%)
    pallas_call x1, Pallas kernels, on_device(): pl.pallas_call(functools.partial(kernel, n, n_cols, R, hops), out_shape=(...  50.4 us
    pallas_call x1, Pallas kernels, on_device(): pl.pallas_call(write_out, out_shape=(out,) * 4, in_specs=[anywhere] * 4,...  2.79 us

commit v1 on v0

--- a/solution.py
+++ b/solution.py
@@ -180,17 +180,22 @@
             def _():
                 frame_copy(h, j).wait_recv()
 
+        def each(values, weight):
+            out = mm(values[0] if len(values) == 1 else jnp.concatenate(values, axis=0), weight)
+            return [out[i * M : (i + 1) * M] for i in range(len(values))]
+
         x2 = [load(a2[cut(j)])]
         if hops > 0:
             arrive(1)
             x2.append(load(x2in[0, cut(j)]))
         t2 = [act(values) for values in x2]
+        u1 = each(t2, u[1])
+        part = u1[0]
+        if hops > 0:
+            part = part + mm(t2[1], u[0])
 
         @pl.when(k == last - 1)
         def _():
-            part = mm(t2[0], u[1])
-            if hops > 0:
-                part = part + mm(t2[1], u[0])
             qs[cut(j)] = part.astype(jnp.bfloat16).reshape(R, W, C)
             part_copy(0, j).start()
 
@@ -198,30 +203,39 @@
             arrive(h)
             x2.append(load(x2in[h - 1, cut(j)]))
             t2.append(act(x2[h]))
+        u2 = each(t2[:3], u[2])
+        if hops > 1:
+            u1 = u1 + each(t2[2:4], u[1])
+            u0 = each(t2[2:5], u[0])
         x3 = []
-        for i in range(min(3, hops + 1)):
-            total = x2[i].astype(jnp.float32) + tb1[...][None, :]
-            for tap in range(3):
-                if i + tap <= hops:
-                    total = total + mm(t2[i + tap], u[2 - tap])
+        for i in range(len(u2)):
+            total = x2[i].astype(jnp.float32) + tb1[...][None, :] + u2[i]
+            if i + 1 < len(u1):
+                total = total + u1[i + 1]
+            if i + 2 <= hops:
+                total = total + u0[i]
             if i > 0:
                 total = jnp.where(k >= i, total, 0.0)
             x3.append(total.astype(jnp.bfloat16))
         t3 = [act(values) for values in x3]
+        v1 = each(t3[:2], v[1])
+        second = v1[0]
+        if len(t3) > 1:
+            v0 = each(t3[1:], v[0])
+            second = second + v0[0]
 
         @pl.when(k == last - 1)
         def _():
-            part = mm(t3[0], v[1])
-            if len(t3) > 1:
-                part = part + mm(t3[1], v[0])
-            ps[cut(j)] = part.astype(jnp.bfloat16).reshape(R, W, C)
+            ps[cut(j)] = second.astype(jnp.bfloat16).reshape(R, W, C)
             part_copy(1, j).start()
 
         a3[cut(j)] = x3[0].reshape(R, W, C)
         out_copy(2, j).start()
-        total = x3[0].astype(jnp.float32) + tb2[...][None, :]
-        for tap in range(len(t3)):
-            total = total + mm(t3[tap], v[2 - tap])
+        total = x3[0].astype(jnp.float32) + tb2[...][None, :] + mm(t3[0], v[2])
+        if len(t3) > 1:
+            total = total + v1[1]
+        if len(t3) > 2:
+            total = total + v0[1]
         a4[cut(j)] = total.astype(jnp.bfloat16).reshape(R, W, C)
         out_copy(3, j).start()
 

time: 54 us -> 54 us (level)
  no operation moved by 1% of the time
where the time goes in v1:
time: 54 us; the launch traced here: 53.8 us
  Pallas kernels  53.2 us (99%)
  between operations  0.64 us (1%)
    pallas_call x1, Pallas kernels, on_device(): pl.pallas_call(functools.partial(kernel, n, n_cols, R, hops), out_shape=(...  50.4 us
    pallas_call x1, Pallas kernels, on_device(): pl.pallas_call(write_out, out_shape=(out,) * 4, in_specs=[anywhere] * 4,...  2.79 us

profile of v1, /device:TPU:25, one launch (start us, length us, event | category | flops | bytes accessed | tf_op | source)
XLA Modules:
  0.0 53.8 jit_solution(6540226973201617358)
XLA Ops:
  0.6 50.4 %shard_map.120 = (bf16[1,48,32,256]{3,2,1,0:T(8,128)(2,1)}, bf16[1,48,32,256]{3,2,1,0:T(8,128)(2,1)}, bf16[1,48,32,256]{3,2,1,0:T(8,128)(2,1)}, bf16[1,48,32,256]{3,2,1,0:T(8,128)(2,1)}) custom-call(bf16[1,48,32,256]{3,2,1,0:T(8,128)(2,1)} %refs_0_.1, bf16[3,768,256]{2,1,0:T(8,128)(2,1)} %bitcast.2, f32[256]{0:T(256)} %refs_2_.1, ...), custom_call_target="tpu_custom_call" | custom-call | tf_op jit(solution)/shard_map/pallas_call | solution.py:345
  51.0 2.8 %shard_map.121 = (bf16[1,48,32,256]{3,2,1,0:T(8,128)(2,1)}, bf16[1,48,32,256]{3,2,1,0:T(8,128)(2,1)}, bf16[1,48,32,256]{3,2,1,0:T(8,128)(2,1)}, bf16[1,48,32,256]{3,2,1,0:T(8,128)(2,1)}) custom-call(bf16[1,48,32,256]{3,2,1,0:T(8,128)(2,1)} %get-tuple-element.8.refs_0_, bf16[1,48,32,256]{3,2,1,0:T(8,128)(2,1)} %get-tuple-element.9.refs_1_, ...), custom_call_target="tpu_custom_call" | custom-call | tf_op jit(solution)/shard_map/pallas_call | solution.py:368
